TPU v7x, 256 devices: a whole 4x4x8 slice. The times are simulated.
256 devices in a mesh: seq: 64 (over y, z, core), tp: 4 (over x).
Axes of the slice: x: 4, y: 4, z: 8, core: 2. Of those that a mesh axis runs over, the one named last changes fastest.
Arguments:
- tokens: bfloat16 [131072, 4096], P('seq', 'tp'), may hold values from -6 to 6
- norm_gain: bfloat16 [4096], replicated, may hold values from 0.25 to 1.75
- router_weight: bfloat16 [4096], replicated, may hold values from -0.09375 to 0.09375
- w_query: bfloat16 [4096, 2048], P(None, 'tp'), may hold values from -1 to 1
- w_key: bfloat16 [4096, 512], P(None, 'tp'), may hold values from -1 to 1
- w_value: bfloat16 [4096, 512], P(None, 'tp'), may hold values from -0.1875 to 0.1875
- w_out: bfloat16 [2048, 4096], P('tp', 'seq'), may hold values from -0.125 to 0.125
- seg_ids: int32 [32], replicated, may hold values from 0 to 63, as said below
- blk_ids: int32 [32, 2], replicated, may hold values from 0 to 15, as said below
Outputs:
- updated: bfloat16 [128, 128, 4096], P('seq', None, 'tp')
Inputs may be any that keep to these rules, and one draw needn't show every extreme that they name: `seg_ids`: Distinct, in increasing order; in every draw all 1 segments of one index of seq are selected, so that one index holds 2 selected blocks. `blk_ids`: each row holds distinct numbers in increasing order.
All inputs are finite; a program needn't handle non-finite values.
Results may differ from a plain program's by a relative error of at most 0.0095.
Values may be sent and summed in bfloat16 or wider, within the bound.
A program may use at most 128 MiB of HBM per device.

v0:
```python
import jax
import jax.numpy as jnp
from jax import lax
from jax.sharding import PartitionSpec as P

HD = 128
BLK = 128
SEG_BLK = 16
PER_SEG = 2
SEG_DEV = 1


far_position = 1073741824


def layer_rows(
    row_data,
    query_pos,
    key_index,
    key_pos,
    norm_gain,
    router_weight,
    w_query,
    w_key,
    w_value,
    w_out,
):
    full_rows = lax.all_gather(row_data, "tp", axis=1, tiled=True)
    floats = full_rows.astype(jnp.float32)
    square_mean = jnp.mean(floats * floats, axis=-1, keepdims=True)
    normed = (floats * lax.rsqrt(square_mean + 1e-05) * norm_gain.astype(jnp.float32)).astype(
        jnp.bfloat16
    )
    gate = jax.nn.sigmoid(jnp.dot(full_rows, router_weight, preferred_element_type=jnp.float32))
    queries = jnp.dot(normed, w_query, preferred_element_type=jnp.float32).astype(jnp.bfloat16)
    key_here = jnp.dot(normed, w_key, preferred_element_type=jnp.float32).astype(jnp.bfloat16)
    value_here = jnp.dot(normed, w_value, preferred_element_type=jnp.float32).astype(jnp.bfloat16)
    key_all, value_all = (
        lax.all_gather(key_here, "seq", axis=0, tiled=True),
        lax.all_gather(value_here, "seq", axis=0, tiled=True),
    )
    key_all = jnp.take(key_all, key_index, axis=0)
    value_all = jnp.take(value_all, key_index, axis=0)
    visible = key_pos[None, :] <= query_pos[:, None]
    local_heads = queries.shape[1] // HD

    def one_head(head):
        query_head = lax.dynamic_slice_in_dim(queries, head * HD, HD, 1)
        scores = jnp.dot(query_head, key_all.T, preferred_element_type=jnp.float32) / jnp.sqrt(
            jnp.float32(HD)
        )
        scores = jnp.where(visible, scores, -jnp.inf)
        weights = jax.nn.softmax(scores, axis=-1).astype(jnp.bfloat16)
        return jnp.dot(weights, value_all, preferred_element_type=jnp.float32).astype(jnp.bfloat16)

    per_head = lax.map(one_head, jnp.arange(local_heads, dtype=jnp.int32))
    heads_out = jnp.transpose(per_head, (1, 0, 2)).reshape(row_data.shape[0], local_heads * HD)
    terms = jnp.dot(
        heads_out,
        lax.all_gather(w_out, "seq", axis=1, tiled=True),
        preferred_element_type=jnp.float32,
    )
    attended = lax.psum_scatter(terms, "tp", scatter_dimension=1, tiled=True)
    return (row_data.astype(jnp.float32) + gate[:, None] * attended).astype(jnp.bfloat16)


def on_device(tokens, norm_gain, router_weight, w_query, w_key, w_value, w_out, seg_ids, blk_ids):
    own_index = lax.axis_index("seq")
    home_blocks = SEG_DEV * SEG_BLK
    slot_count = SEG_DEV * PER_SEG
    local_cols = tokens.shape[1]
    blocks = (seg_ids[:, None] * SEG_BLK + blk_ids).reshape(-1)
    block_count = blocks.shape[0]
    homes = blocks // home_blocks
    ranks = jnp.arange(block_count, dtype=jnp.int32)
    slots = ranks - jnp.sum((homes[None, :] < homes[:, None]).astype(jnp.int32), axis=1)
    slot_numbers = jnp.arange(slot_count, dtype=jnp.int32)
    matches = (homes[None, :] == own_index) & (slots[None, :] == slot_numbers[:, None])
    filled = jnp.any(matches, axis=1)
    local_block = jnp.sum(jnp.where(matches, blocks[None, :] % home_blocks, 0), axis=1)
    block_rows = tokens.reshape(home_blocks, BLK, local_cols)
    mine = jnp.take(block_rows, local_block, axis=0)
    offsets = jnp.arange(BLK, dtype=jnp.int32)
    weights_all = (norm_gain, router_weight, w_query, w_key, w_value, w_out)
    row_data = mine.reshape(slot_count * BLK, local_cols)
    starts = (own_index * home_blocks + local_block) * BLK
    query_pos = jnp.where(
        filled[:, None], starts[:, None] + offsets[None, :], far_position
    ).reshape(-1)
    key_index = ((homes * slot_count + slots)[:, None] * BLK + offsets[None, :]).reshape(-1)
    key_pos = (blocks[:, None] * BLK + offsets[None, :]).reshape(-1)
    new_rows = layer_rows(row_data, query_pos, key_index, key_pos, *weights_all)
    updated = jnp.where(
        filled[:, None, None],
        new_rows.reshape(slot_count, BLK, local_cols),
        jnp.zeros((), jnp.bfloat16),
    )
    return updated


def solution(mesh):
    placed = (
        P("seq", "tp"),
        P(),
        P(),
        P(None, "tp"),
        P(None, "tp"),
        P(None, "tp"),
        P("tp", "seq"),
        P(),
        P(),
    )
    return jax.shard_map(
        on_device, mesh=mesh, in_specs=placed, out_specs=P("seq", None, "tp"), check_vma=False
    )
```

profile of v0, /device:TPU:2, one launch (start us, length us, event | category | flops | bytes accessed | tf_op | source)
XLA Modules:
  0.0 351.6 jit_solution(12752545335056323452)
XLA Ops:
  6.5 0.7 broadcast_multiply_fusion.1
  7.3 0.7 broadcast_add_fusion
  8.2 0.2 convert_reduce_fusion
  8.6 2.8 gather_fusion
  11.4 1.0 bitcast_select_fusion
  12.4 0.7 convert_element_type.36
  13.1 34.8 %all-gather.5.cloned.1.call-done = bf16[256,4096]{1,0:T(8,128)(2,1)} async-done(((bf16[256,1024]{1,0:T(8,128)(2,1)}), bf16[256,4096]{1,0:T(8,128)(2,1)}) %all-gather.5.cloned.1.call-update) | async-done | bytes 2097168 | tf_op jit(solution)/shard_map/all_gather | solution.py:28
  47.9 2.2 fusion.9
  50.2 3.0 convolution_convert_fusion.2
  53.3 2.7 convolution_convert_fusion.1
  56.0 0.5 all-gather.11.cloned.1.call-update
  56.5 0.2 reduce-scatter.2.cloned.1.call-start
  57.1 0.7 add_bitcast_fusion
  57.8 4.2 %convolution_convert_fusion = bf16[256,512]{1,0:T(8,128)(2,1)} fusion(bf16[4096,512]{1,0:T(8,128)(2,1)} %param.16, bf16[256,4096]{1,0:T(8,128)(2,1)S(1)} %copy-done.1, f32[4096]{0:T(1024)S(1)} %convert_element_type.36, f32[256]{0:T(256)S(1)} %add_rsqrt_fusion), kind=kOutput, calls=%fused_computation.22 | convolution fusion | flops 1078067200 | bytes 6571008 | tf_op jit(solution)/shard_map/dot_general | solution.py:35
  62.0 71.4 %all-gather.7.cloned.1.call-done = bf16[16384,128]{1,0:T(8,128)(2,1)} async-done(((bf16[256,128]{1,0:T(8,128)(2,1)}), bf16[16384,128]{1,0:T(8,128)(2,1)}) %all-gather.7.cloned.1.call-update) | async-done | bytes 4194320 | tf_op jit(solution)/shard_map/all_gather | solution.py:39
  133.4 24.6 %gather_fusion.1 = bf16[8192,128]{1,0:T(8,128)(2,1)S(1)} fusion(bf16[16384,128]{1,0:T(8,128)(2,1)} %all-gather.7.cloned.1.call-done, s32[8192]{0:T(1024)S(1)} %fusion.12), kind=kCustom, calls=%fused_computation.clone | custom fusion | bytes 4227072 | tf_op jit(solution)/shard_map/jit(_take)/gather | solution.py:42
  158.0 54.6 %all-gather.9.cloned.1.call-done = bf16[16384,128]{1,0:T(8,128)(2,1)} async-done(((bf16[256,128]{1,0:T(8,128)(2,1)}), bf16[16384,128]{1,0:T(8,128)(2,1)}) %all-gather.9.cloned.1.call-update) | async-done | bytes 4194320 | tf_op jit(solution)/shard_map/all_gather | solution.py:40
  212.6 30.7 %gather_fusion.2 = bf16[8192,128]{1,0:T(8,128)(2,1)} fusion(bf16[16384,128]{1,0:T(8,128)(2,1)} %all-gather.9.cloned.1.call-done, s32[8192]{0:T(1024)S(1)} %fusion.12), kind=kCustom, calls=%fused_computation.1.clone | custom fusion | bytes 4227072 | tf_op jit(solution)/shard_map/jit(_take)/gather | solution.py:43
  243.2 7.0 %broadcast_select_fusion = (bf16[8192,128]{1,0:T(8,128)(2,1)}, bf16[8192,128]{1,0:T(8,128)(2,1)}) fusion(bf16[8192,128]{1,0:T(8,128)(2,1)} %gather_fusion.2, pred[8192]{0:T(1024)(128)(4,1)S(1)} %fusion.15, bf16[8192,128]{1,0:T(8,128)(2,1)S(1)} %gather_fusion.1), kind=kLoop, calls=%fused_computation.20 | loop fusion | flops 2097152 | bytes 8396800 | tf_op jit(solution)/shard_map/jit(_take)/select_n | solution.py:43
  250.2 32.1 %while.11 = (s32[]{:T(128)}, bf16[4,256,128]{1,2,0:T(8,128)(2,1)S(1)}, s32[4]{0:T(128)S(1)}, bf16[256,512]{1,0:T(8,128)(2,1)}, bf16[8192,128]{1,0:T(8,128)(2,1)}...) while((s32[]{:T(128)}, ...), condition=%wide.region_7.9_spmd.clone, body=%wide.region_4.8_spmd.clone.sunk | while | flops 1092648448 | bytes 38181076 | solution.py:56
  250.2 0.6 dynamic_slice.16
  251.4 3.1 fusion.40
  254.5 1.3 fusion.41
  255.9 0.2 copy-done.4
  256.1 1.9 fusion.42
  258.2 0.6 dynamic_slice.16
  259.4 3.1 fusion.40
  262.5 1.3 fusion.41
  263.8 0.2 copy-done.4
  264.1 1.9 fusion.42
  266.2 0.6 dynamic_slice.16
  267.4 3.2 fusion.40
  270.6 1.4 fusion.41
  271.9 0.2 copy-done.4
  272.2 1.9 fusion.42
  274.2 0.6 dynamic_slice.16
  275.5 3.1 fusion.40
  278.6 1.3 fusion.41
  280.0 0.3 copy-done.4
  280.2 1.9 fusion.42
  282.3 9.2 %all-gather.11.cloned.1.call-done = bf16[512,4096]{0,1:T(8,128)(2,1)} async-done(((bf16[512,64]{0,1:T(8,128)(2,1)}), bf16[512,4096]{0,1:T(8,128)(2,1)}) %all-gather.11.cloned.1.call-update) | async-done | bytes 4194320 | tf_op jit(solution)/shard_map/all_gather | solution.py:60
  291.5 5.5 %fusion.23 = f32[256,4096]{1,0:T(8,128)} fusion(bf16[256,512]{0,1:T(8,128)(2,1)S(1)} %bitcast.53, bf16[512,4096]{0,1:T(8,128)(2,1)} %all-gather.11.cloned.1.call-done), kind=kOutput, calls=%fused_computation.61 | convolution fusion | flops 1073741824 | bytes 8650752 | tf_op jit(solution)/shard_map/dot_general | solution.py:58
  297.0 0.7 copy-done.5
  297.7 0.9 copy-done.2
  298.6 0.6 fusion.22
  299.3 43.3 %reduce-scatter.2.cloned.1.call-done = f32[256,1024]{1,0:T(8,128)} async-done(((f32[256,4096]{1,0:T(8,128)}), f32[256,1024]{1,0:T(8,128)}) %reduce-scatter.2.cloned.1.call-update) | async-done | bytes 1048592 | tf_op jit(solution)/shard_map/reduce_scatter | solution.py:63
  342.6 1.6 add_convert_fusion
  344.2 0.9 broadcast_select_fusion.2
  (47 shorter events, 1.5 us)
Async XLA Ops:
  6.5 43.6 %copy-start = (bf16[4096,128]{1,0:T(8,128)(2,1)S(1)}, bf16[4096,128]{1,0:T(8,128)(2,1)}, u32[]{:S(2)}) copy-start(bf16[4096,128]{1,0:T(8,128)(2,1)} %param.17) | copy-start | bytes 3145732
  6.5 41.4 %all-gather.5.cloned.1.call-start = ((), (), s32[]{:S(2)}) async-start(), calls=%async_computation.1 | async-start | bytes 2621440 | tf_op jit(solution)/shard_map/all_gather | solution.py:28
  11.4 1.7 copy-start.3
  12.4 121.0 %all-gather.7.cloned.1.call-start = ((), (), s32[]{:S(2)}) async-start(), calls=%async_computation.2 | async-start | bytes 4259840 | tf_op jit(solution)/shard_map/all_gather | solution.py:39
  47.9 5.3 %copy-start.1 = (bf16[256,4096]{1,0:T(8,128)(2,1)S(1)}, bf16[256,4096]{1,0:T(8,128)(2,1)}, u32[]{:S(2)}) copy-start(bf16[256,4096]{1,0:T(8,128)(2,1)} %all-gather.5.cloned.1.call-done) | copy-start | bytes 6291460
  53.2 159.4 %all-gather.9.cloned.1.call-start = ((), (), s32[]{:S(2)}) async-start(), calls=%async_computation.3 | async-start | bytes 4259840 | tf_op jit(solution)/shard_map/all_gather | solution.py:40
  56.0 235.6 %all-gather.11.cloned.1.call-start = ((), (), s32[]{:S(2)}) async-start(), calls=%async_computation.4 | async-start | bytes 4259840 | tf_op jit(solution)/shard_map/all_gather | solution.py:60
  56.5 286.0 %reduce-scatter.2.cloned.1.call-start = ((), (), s32[]{:S(2)}) async-start(), calls=%async_computation.5 | async-start | bytes 5242880 | tf_op jit(solution)/shard_map/reduce_scatter | solution.py:63
  254.5 1.6 copy-start.4
  262.5 1.6 copy-start.4
  270.6 1.6 copy-start.4
  278.6 1.6 copy-start.4
  297.0 0.7 copy-start.5
  297.0 1.6 copy-start.2
Sparse Core Ops, SparseCore 0:
  12.5 35.3 all-gather.4
  53.3 80.0 all-gather.6
  136.2 76.3 all-gather.8
  215.2 76.3 all-gather.10
  297.2 45.3 reduce-scatter.1
where the time goes:
time: 355 us; the launch traced here: 352 us
  waiting for transfers between devices  214 us (60%)
  local copies, waits for them, and re-layouts  63.7 us (18%)
  matrix products  36.2 us (10%)
  other arithmetic  21.6 us (6%)
  between operations  13.3 us (4%)
    all_gather x1, waiting for transfers between devices, layer_rows(): lax.all_gather(key_here, 'seq', axis=0, tiled=True)  71.4 us
    all_gather x1, waiting for transfers between devices, layer_rows(): lax.all_gather(value_here, 'seq', axis=0, tiled=True)  54.6 us
    reduce_scatter x1, waiting for transfers between devices, layer_rows(): attended = lax.psum_scatter(terms, 'tp', scatter_dimension=1, tiled=True)  43.3 us
    all_gather x1, waiting for transfers between devices, layer_rows(): full_rows = lax.all_gather(row_data, 'tp', axis=1, tiled=True)  34.8 us
    gather x1, local copies, waits for them, and re-layouts, layer_rows(): value_all = jnp.take(value_all, key_index, axis=0)  30.7 us
    gather x1, local copies, waits for them, and re-layouts, layer_rows(): key_all = jnp.take(key_all, key_index, axis=0)  24.6 us
    dot_general x4, matrix products, one_head(): jnp.dot(query_head, key_all.T, preferred_element_type=jnp.float32)  12.5 us
    all_gather x1, waiting for transfers between devices, layer_rows(): lax.all_gather(w_out, 'seq', axis=1, tiled=True)  9.24 us
  transfers between devices with their start and end apart: 5, of which 5 were waited for; matrix products, arithmetic and copies ran while one was open for 28% of the time, Pallas kernels for 0%

commit v1 on v0

v1 whole, which is shorter than its diff:
```python
import functools

import jax
import jax.numpy as jnp
from jax import lax
from jax.experimental import pallas as pl
from jax.experimental.pallas import tpu as pltpu
from jax.sharding import PartitionSpec as P

MESH = pl.DeviceIdType.MESH
F32 = jnp.float32
BF16 = jnp.bfloat16

NY, NZ, NX = 4, 8, 4
HD = 128
BLK = 128
LOCAL_HEADS = 4
ROWS = 2 * BLK
QROWS = LOCAL_HEADS * BLK
FEATS = 1024
SEGS = 32
KEY_SEGS = 4
LOG2E = 1.4426950408889634
Q_SCALE = LOG2E / (128.0**0.5)
MASKED = -1e30

Y_FIRST = 96
PY, PZ, RZ, RY, SIB, COPIES = 0, 4, 12, 20, 44, 56


def dot(a, b):
    return jnp.dot(a, b, preferred_element_type=F32)


def dot_t(a, b):
    return lax.dot_general(a, b, (((1,), (1,)), ((), ())), preferred_element_type=F32)


class Place:
    def __init__(self):
        s = lax.axis_index("seq")
        self.x = lax.axis_index("tp")
        self.s = s
        self.y = s // (NZ * 2)
        self.z = (s // 2) % NZ
        self.c = s % 2

    def at(self, x=None, y=None, z=None, c=None):
        x = self.x if x is None else x
        y = self.y if y is None else y
        z = self.z if z is None else z
        c = self.c if c is None else c
        return (y * (NZ * 2) + z * 2 + c, x)


class Copies:
    def __init__(self, send_sems, recv_sems):
        self.ss, self.rs = send_sems, recv_sems
        self.made = {}

    def send(self, src, dst, k, device):
        copy = pltpu.make_async_remote_copy(
            src_ref=src,
            dst_ref=dst,
            send_sem=self.ss.at[k],
            recv_sem=self.rs.at[k],
            device_id=device,
            device_id_type=MESH,
        )
        copy.start()
        self.made[k] = copy

    def recv(self, k):
        self.made[k].wait_recv()

    def drain(self):
        for copy in self.made.values():
            copy.wait_send()
        self.made = {}


def gather_yz(me, both, cp):
    buf, other = both.at[0], both.at[1]
    up_y, down_y = me.at(y=(me.y + 1) % NY), me.at(y=(me.y + 3) % NY)
    up_z, down_z = me.at(z=(me.z + 1) % NZ), me.at(z=(me.z + 7) % NZ)
    sib = me.at(c=1 - me.c)
    half = Y_FIRST // 2
    mid = Y_FIRST + (256 - Y_FIRST) // 2

    def p(dy, lo=0, hi=Y_FIRST):
        return buf.at[dy, 0, lo:hi]

    def col(dz, lo=0, hi=Y_FIRST):
        return buf.at[:, dz, lo:hi]

    def r(dz, dy=0, lo=Y_FIRST, hi=256):
        return buf.at[dy, dz, lo:hi]

    order = (0, 7, 1, 6, 2, 5, 3, 4)

    def row_out(j):
        cp.send(r(order[j]), r(order[j], 3), RY + j, up_y)
        cp.send(r(order[j]), r(order[j], 1), RY + 8 + j, down_y)

    def row_in(j):
        cp.recv(RY + j)
        if j % 2 == 0:
            cp.send(r(order[j], 3), r(order[j], 2), RY + 16 + j, up_y)
        cp.recv(RY + 8 + j)
        if j % 2 == 1:
            cp.send(r(order[j], 1), r(order[j], 2), RY + 16 + j, down_y)

    def sib_col(j, dz):
        cp.send(col(dz), other.at[:, dz, 0:Y_FIRST], SIB + j, sib)

    def sib_row(j, dy):
        cp.send(buf.at[dy, :, Y_FIRST:256], other.at[dy, :, Y_FIRST:256], SIB + 8 + j, sib)

    cp.send(p(0), p(3), PY, up_y)
    cp.send(p(0), p(1), PY + 1, down_y)
    cp.send(r(0), r(7), RZ, up_z)
    cp.send(r(0), r(1), RZ + 1, down_z)
    row_out(0)
    yield
    cp.recv(PY)
    cp.send(p(3, 0, half), p(2, 0, half), PY + 2, up_y)
    cp.recv(PY + 1)
    cp.send(p(1, half, Y_FIRST), p(2, half, Y_FIRST), PY + 3, down_y)
    yield
    cp.recv(RZ)
    cp.send(r(7), r(6), RZ + 2, up_z)
    cp.recv(RZ + 1)
    cp.send(r(1), r(2), RZ + 3, down_z)
    row_out(1)
    row_out(2)
    yield
    cp.recv(PY + 2)
    cp.recv(PY + 3)
    cp.send(col(0), col(7), PZ, up_z)
    cp.send(col(0), col(1), PZ + 1, down_z)
    sib_col(0, 0)
    yield
    cp.recv(RZ + 2)
    cp.send(r(6), r(5), RZ + 4, up_z)
    cp.recv(RZ + 3)
    cp.send(r(2), r(3), RZ + 5, down_z)
    row_out(3)
    row_out(4)
    yield
    row_in(0)
    cp.recv(RZ + 4)
    cp.send(r(5, 0, Y_FIRST, mid), r(4, 0, Y_FIRST, mid), RZ + 6, up_z)
    cp.recv(RZ + 5)
    cp.send(r(3, 0, mid, 256), r(4, 0, mid, 256), RZ + 7, down_z)
    row_out(5)
    row_out(6)
    yield
    cp.recv(PZ)
    cp.send(col(7), col(6), PZ + 2, up_z)
    cp.recv(PZ + 1)
    cp.send(col(1), col(2), PZ + 3, down_z)
    sib_col(1, 7)
    sib_col(2, 1)
    yield
    cp.recv(RZ + 6)
    cp.recv(RZ + 7)
    row_out(7)
    sib_row(0, 0)
    row_in(1)
    row_in(2)
    yield
    cp.recv(PZ + 2)
    cp.send(col(6), col(5), PZ + 4, up_z)
    cp.recv(PZ + 3)
    cp.send(col(2), col(3), PZ + 5, down_z)
    sib_col(3, 6)
    sib_col(4, 2)
    row_in(3)
    row_in(4)
    yield
    cp.recv(PZ + 4)
    cp.send(col(5, 0, half), col(4, 0, half), PZ + 6, up_z)
    cp.recv(PZ + 5)
    cp.send(col(3, half, Y_FIRST), col(4, half, Y_FIRST), PZ + 7, down_z)
    sib_col(5, 5)
    sib_col(6, 3)
    row_in(5)
    yield
    row_in(6)
    row_in(7)
    sib_row(1, 3)
    sib_row(2, 1)
    yield
    cp.recv(PZ + 6)
    cp.recv(PZ + 7)
    sib_col(7, 4)
    for j in range(8):
        cp.recv(RY + 16 + j)
    sib_row(3, 2)
    yield
    for j in range(12):
        cp.recv(SIB + j)
    cp.drain()


def ring_x(me, buf, cp, base):
    mid = BLK // 2
    up, down = me.at(x=(me.x + 1) % NX), me.at(x=(me.x + 3) % NX)
    cp.send(buf.at[0], buf.at[3], base, up)
    cp.send(buf.at[0], buf.at[1], base + 1, down)
    yield
    cp.recv(base)
    cp.send(buf.at[3, 0:mid], buf.at[2, 0:mid], base + 2, up)
    cp.recv(base + 1)
    cp.send(buf.at[1, mid:BLK], buf.at[2, mid:BLK], base + 3, down)
    yield
    cp.recv(base + 2)
    cp.recv(base + 3)


def run(steps, count=None):
    if count is None:
        for _ in steps:
            pass
        return
    for _ in range(count):
        next(steps, None)


def kernel(
    seg_ref,
    blk_ref,
    gain_ref,
    router_ref,
    tok_ref,
    wq_hbm,
    wk_hbm,
    wv_hbm,
    wo_ref,
    out_ref,
    tok,
    wq,
    wk,
    wv,
    wkv,
    xg0,
    xg1,
    normed,
    wsend,
    wrecv,
    wg,
    kv0,
    kv1,
    qx,
    acc,
    top,
    gates,
    hg0,
    hg1,
    att,
    local_sems,
    w_ss,
    w_rs,
    gw_ss,
    gw_rs,
    g0_ss,
    g0_rs,
    g1_ss,
    g1_rs,
    x_ss,
    x_rs,
):
    me = Place()
    x, y, z, c = me.x, me.y, me.z, me.c
    xg, hg = (xg0, xg1), (hg0, hg1)
    tok_copy = pltpu.make_async_copy(tok_ref, tok, local_sems.at[0])
    wk_copy = pltpu.make_async_copy(wk_hbm, wk, local_sems.at[1])
    wv_copy = pltpu.make_async_copy(wv_hbm, wv, local_sems.at[2])
    wq_copy = pltpu.make_async_copy(wq_hbm, wq, local_sems.at[3])
    for copy in (tok_copy, wk_copy, wv_copy, wq_copy):
        copy.start()

    sib = me.at(c=1 - c)
    barrier = pltpu.get_barrier_semaphore()
    neighbours = [
        me.at(x=(x + 1) % NX),
        me.at(x=(x + 3) % NX),
        me.at(y=(y + 1) % NY),
        me.at(y=(y + 3) % NY),
        me.at(z=(z + 1) % NZ),
        me.at(z=(z + 7) % NZ),
        sib,
    ]
    for device in neighbours:
        pl.semaphore_signal(barrier, 1, device_id=device, device_id_type=MESH)

    @pl.when(x != y)
    def _():
        for h in range(2):
            pl.semaphore_signal(
                barrier, 1, device_id=me.at(x=y, y=x, c=h), device_id_type=MESH
            )

    here = lax.broadcasted_iota(jnp.int32, (64, 128), 1)
    there = lax.broadcasted_iota(jnp.int32, (64, 128), 0)
    spread = jnp.where(here == there + 64 * c, 1.0, 0.0).astype(BF16)
    for h in range(2):
        wsend[h] = dot(wo_ref[h * 256 : (h + 1) * 256, :], spread).astype(BF16)

    own = me.s

    def look(j, carry):
        rank, hit, first, second = carry
        seg = seg_ref[j]
        same = seg == own
        return (
            rank + jnp.where(seg < own, 1, 0),
            jnp.where(same, 1, hit),
            jnp.where(same, blk_ref[j, 0], first),
            jnp.where(same, blk_ref[j, 1], second),
        )

    zero = jnp.int32(0)
    rank, filled, first, second = lax.fori_loop(0, SEGS, look, (zero, zero, zero, zero))

    tok_copy.wait()
    for s, block in enumerate((first, second)):
        xg[s][0] = tok[block]

    @pl.when(x != y)
    def _():
        pl.semaphore_wait(barrier, 9)

    @pl.when(x == y)
    def _():
        pl.semaphore_wait(barrier, 7)

    xcp = Copies(x_ss, x_rs)
    x0 = ring_x(me, xg0, xcp, 0)
    x1 = ring_x(me, xg1, xcp, 4)
    run(x0, 1)

    def w_copy(h, slot, device):
        return pltpu.make_async_remote_copy(
            src_ref=wsend.at[h],
            dst_ref=wrecv.at[slot],
            send_sem=w_ss.at[h],
            recv_sem=w_rs.at[slot],
            device_id=device,
            device_id_type=MESH,
        )

    @pl.when(x != y)
    def _():
        for h in range(2):
            w_copy(h, c, me.at(x=y, y=x, c=h)).start()

    @pl.when(x == y)
    def _():
        w_copy(1 - c, c, sib).start()
        wrecv[c] = wsend[c]

    wk_copy.wait()
    wv_copy.wait()
    wkv[:, :, 0:HD] = wk[...]
    wkv[:, :, HD : 2 * HD] = wv[...]

    @pl.when(x != y)
    def _():
        for h in range(2):
            w_copy(h, h, me.at(x=y, y=x, c=h)).wait()

    @pl.when(x == y)
    def _():
        w_copy(1 - c, 1 - c, sib).wait()

    wg[0, 0, 0] = wrecv[0] + wrecv[1]
    gw = gather_yz(me, wg, Copies(gw_ss, gw_rs))
    run(gw, 3)

    run(x0, 1)
    run(x1, 1)
    run(gw, 2)

    feat = [(x + d) % NX for d in range(NX)]

    def norm(s):
        rows = slice(s * BLK, (s + 1) * BLK)
        squares = jnp.zeros((BLK, 1), F32)
        routed = jnp.zeros((BLK, 1), F32)
        for d in range(NX):
            part = xg[s][d].astype(F32)
            squares += jnp.sum(part * part, axis=1, keepdims=True)
            routed += jnp.sum(part * router_ref[feat[d]].astype(F32), axis=1, keepdims=True)
        scale = lax.rsqrt(squares * (1.0 / (NX * FEATS)) + 1e-05)
        gates[rows] = jax.nn.sigmoid(routed)
        for d in range(NX):
            normed[d] = (xg[s][d].astype(F32) * scale * gain_ref[feat[d]].astype(F32)).astype(BF16)

    def through(weight):
        total = dot(normed[0], weight[feat[0]])
        for d in range(1, NX):
            total += dot(normed[d], weight[feat[d]])
        return total.astype(BF16)

    def keys(kv):
        found = through(wkv)
        kv[0, 0, 0] = jnp.concatenate([found[:, 0:HD], found[:, HD : 2 * HD]], axis=0)

    def queries(s):
        found = through(wq).astype(F32) * Q_SCALE
        high = found.astype(BF16)
        low = (found - high.astype(F32)).astype(BF16)
        for h in range(LOCAL_HEADS):
            rows = slice(s * QROWS + h * BLK, s * QROWS + (h + 1) * BLK)
            qx[rows, 0:HD] = high[:, h * HD : (h + 1) * HD]
            qx[rows, HD : 2 * HD] = low[:, h * HD : (h + 1) * HD]

    ones = jnp.ones((BLK, HD), BF16)

    def twice(key):
        return jnp.concatenate([key, key], axis=1)

    run(x0)
    norm(0)
    keys(kv0)
    g0 = gather_yz(me, kv0, Copies(g0_ss, g0_rs))
    run(g0, 1)
    wq_copy.wait()
    queries(0)
    run(g0, 2)
    run(gw, 2)
    run(x1, 1)
    run(g0, 1)
    run(gw, 2)
    run(g0, 1)
    run(gw, 2)
    run(g0, 1)
    run(gw)
    run(x1)
    norm(1)
    keys(kv1)
    g1 = gather_yz(me, kv1, Copies(g1_ss, g1_rs))
    run(g1, 1)
    run(g0, 1)
    queries(1)
    run(g0, 1)
    run(g1, 1)

    def own_blocks():
        own0, own1 = kv0[0, 0, 0], kv1[0, 0, 0]
        key0, value0 = own0[0:BLK], own0[BLK : 2 * BLK]
        key1, value1 = own1[0:BLK], own1[BLK : 2 * BLK]
        row = lax.broadcasted_iota(jnp.int32, (QROWS, BLK), 0) % BLK
        column = lax.broadcasted_iota(jnp.int32, (QROWS, BLK), 1)
        seen = column <= row
        q0, q1 = qx[0:QROWS], qx[QROWS : 2 * QROWS]
        s00 = jnp.where(seen, dot_t(q0, twice(key0)), MASKED)
        most = jnp.max(s00, axis=1, keepdims=True)
        top[0:QROWS] = most
        acc[0:QROWS] = dot(
            jnp.exp2(s00 - most).astype(BF16), jnp.concatenate([value0, ones], axis=1)
        )
        s10 = dot_t(q1, twice(key0))
        s11 = jnp.where(seen, dot_t(q1, twice(key1)), MASKED)
        most = jnp.max(jnp.maximum(s10, s11), axis=1, keepdims=True)
        top[QROWS : 2 * QROWS] = most
        acc[QROWS : 2 * QROWS] = dot(
            jnp.exp2(s10 - most).astype(BF16), jnp.concatenate([value0, ones], axis=1)
        ) + dot(jnp.exp2(s11 - most).astype(BF16), jnp.concatenate([value1, ones], axis=1))

    own_blocks()
    run(g0, 1)
    run(g1, 2)
    run(g0, 1)
    run(g1, 1)
    run(g0, 1)
    run(g1, 1)
    run(g0)

    stand_in = jnp.broadcast_to(kv0[0, 0, 0][0:1], (BLK, HD))
    nothing = jnp.zeros((BLK, HD), BF16)

    def attend(kv, chunk):
        key_parts, value_parts = [], []
        for i in range(KEY_SEGS):
            j = chunk * KEY_SEGS + i
            home = seg_ref[j]
            block = kv[(home + c) & 1, ((home >> 4) + NY - y) & 3, ((home >> 1) + NZ - z) & 7]
            seen = j < rank
            key_parts.append(twice(jnp.where(seen, block[0:BLK], stand_in)))
            value_parts.append(
                jnp.concatenate(
                    [
                        jnp.where(seen, block[BLK : 2 * BLK], nothing),
                        jnp.where(seen, ones, nothing),
                    ],
                    axis=1,
                )
            )
        key_chunk = jnp.concatenate(key_parts, axis=0)
        value_chunk = jnp.concatenate(value_parts, axis=0)
        tile = 256
        for t in range(2 * QROWS // tile):
            rows = slice(t * tile, (t + 1) * tile)
            scores = dot_t(qx[rows], key_chunk)
            old = top[rows]
            new = jnp.maximum(old, jnp.max(scores, axis=1, keepdims=True))
            top[rows] = new
            weights = jnp.exp2(scores - new).astype(BF16)
            acc[rows] = acc[rows] * jnp.exp2(old - new) + dot(weights, value_chunk)

    def attend_some(kv, low, high):
        def step(chunk, carry):
            attend(kv, chunk)
            return carry

        lax.fori_loop(low, high, step, 0)

    chunks = SEGS // KEY_SEGS
    for low in range(0, chunks, 2):
        attend_some(kv0, low, low + 2)
        run(g1, 2)
    run(g1)
    attend_some(kv1, 0, chunks)

    h0 = ring_x(me, hg0, xcp, 8)
    h1 = ring_x(me, hg1, xcp, 12)

    def finish(s):
        parts = []
        for h in range(LOCAL_HEADS):
            rows = slice(s * QROWS + h * BLK, s * QROWS + (h + 1) * BLK)
            parts.append((acc[rows, 0:HD] / acc[rows, HD : 2 * HD]).astype(BF16))
        hg[s][0] = jnp.concatenate(parts, axis=1)

    finish(0)
    run(h0, 1)
    finish(1)
    run(h1, 1)

    def project(d, begin):
        heads = jnp.concatenate([hg0[d], hg1[d]], axis=0)
        dy = (x + d + NY - y) % NY
        for j in range(NZ // 2):
            weight = jnp.concatenate(
                [
                    jnp.concatenate(
                        [wg[(k + c) % 2, dy, (2 * j + i + NZ - z) % NZ] for i in range(2)], axis=1
                    )
                    for k in range(2)
                ],
                axis=0,
            )
            lanes = slice(j * 256, (j + 1) * 256)
            term = dot(heads, weight)
            att[:, lanes] = term if begin else att[:, lanes] + term

    project(0, True)
    run(h0, 1)
    run(h1, 1)
    project(3, False)
    project(1, False)
    run(h0)
    run(h1)
    project(2, False)
    own_rows = jnp.concatenate([xg0[0], xg1[0]], axis=0)
    new_rows = own_rows.astype(F32) + gates[...] * att[...]
    out_ref[...] = jnp.where(filled == 1, new_rows, 0.0).astype(BF16)
    xcp.drain()


def on_device(tokens, norm_gain, router_weight, w_query, w_key, w_value, w_out, seg_ids, blk_ids):
    any_space = pl.BlockSpec(memory_space=pl.ANY)
    vmem = pl.BlockSpec(memory_space=pltpu.VMEM)
    smem = pl.BlockSpec(memory_space=pltpu.SMEM)
    dma = pltpu.SemaphoreType.DMA
    new_rows = pl.pallas_call(
        kernel,
        out_shape=jax.ShapeDtypeStruct((ROWS, FEATS), BF16),
        in_specs=[smem, smem, vmem, vmem, any_space, any_space, any_space, any_space, vmem],
        out_specs=vmem,
        scratch_shapes=[
            pltpu.VMEM((16, BLK, FEATS), BF16),
            pltpu.VMEM((NX, FEATS, 512), BF16),
            pltpu.VMEM((NX, FEATS, HD), BF16),
            pltpu.VMEM((NX, FEATS, HD), BF16),
            pltpu.VMEM((NX, FEATS, 2 * HD), BF16),
            pltpu.VMEM((NX, BLK, FEATS), BF16),
            pltpu.VMEM((NX, BLK, FEATS), BF16),
            pltpu.VMEM((NX, BLK, FEATS), BF16),
            pltpu.VMEM((2, 256, 128), BF16),
            pltpu.VMEM((2, 256, 128), BF16),
            pltpu.VMEM((2, NY, NZ, 256, 128), BF16),
            pltpu.VMEM((2, NY, NZ, 256, 128), BF16),
            pltpu.VMEM((2, NY, NZ, 256, 128), BF16),
            pltpu.VMEM((2 * QROWS, 2 * HD), BF16),
            pltpu.VMEM((2 * QROWS, 2 * HD), F32),
            pltpu.VMEM((2 * QROWS, 1), F32),
            pltpu.VMEM((ROWS, 1), F32),
            pltpu.VMEM((NX, BLK, 512), BF16),
            pltpu.VMEM((NX, BLK, 512), BF16),
            pltpu.VMEM((ROWS, FEATS), F32),
            dma((4,)),
            dma((2,)),
            dma((2,)),
            dma((COPIES,)),
            dma((COPIES,)),
            dma((COPIES,)),
            dma((COPIES,)),
            dma((COPIES,)),
            dma((COPIES,)),
            dma((16,)),
            dma((16,)),
        ],
        compiler_params=pltpu.CompilerParams(
            collective_id=0, has_side_effects=True, vmem_limit_bytes=56 << 20
        ),
        name="depth_layer",
    )(
        seg_ids,
        blk_ids,
        norm_gain.reshape(NX, 1, FEATS),
        router_weight.reshape(NX, 1, FEATS),
        tokens.reshape(16, BLK, FEATS),
        w_query.reshape(NX, FEATS, 512),
        w_key.reshape(NX, FEATS, HD),
        w_value.reshape(NX, FEATS, HD),
        w_out,
    )
    return new_rows.reshape(2, BLK, FEATS)


def solution(mesh):
    placed = (
        P("seq", "tp"),
        P(),
        P(),
        P(None, "tp"),
        P(None, "tp"),
        P(None, "tp"),
        P("tp", "seq"),
        P(),
        P(),
    )
    return jax.shard_map(
        on_device, mesh=mesh, in_specs=placed, out_specs=P("seq", None, "tp"), check_vma=False
    )
```

time: 355 us -> 128 us (0.36)
  waiting for transfers between devices: 214 us -> 0 us
  Pallas kernels: 0 us -> 120 us
  local copies, waits for them, and re-layouts: 63.7 us -> 7.44 us
  matrix products: 36.2 us -> 0 us
  other arithmetic: 21.6 us -> 0 us
  between operations: 13.3 us -> 0.01 us
    all_gather x4 -> x0, waiting for transfers between devices: 170 us -> none  [the longest x1 71.4 us: layer_rows(): lax.all_gather(key_here, 'seq', axis=0, tiled=True)]
    pallas_call x0 -> x1, Pallas kernels: none -> 120 us  [on_device(): pl.pallas_call(kernel, out_shape=jax.ShapeDtypeStruct((ROWS, FEATS), BF16...]
    gather x3 -> x0, local copies, waits for them, and re-layouts: 58 us -> none  [the longest x1 30.7 us: layer_rows(): value_all = jnp.take(value_all, key_index, axis=0)]
    reduce_scatter x1 -> x0, waiting for transfers between devices: 43.3 us -> none  [layer_rows(): attended = lax.psum_scatter(terms, 'tp', scatter_dimension=1, tiled=True)]
    dot_general x13 -> x0, matrix products: 36.2 us -> none  [the longest x4 12.5 us: one_head(): jnp.dot(query_head, key_all.T, preferred_element_type=jnp.float32)]
    select_n x5 -> x0, other arithmetic: 8.94 us -> none  [the longest x1 7.01 us: layer_rows(): value_all = jnp.take(value_all, key_index, axis=0)]
    reduce_sum x7 -> x0, other arithmetic: 7.92 us -> none  [the longest x4 5.4 us: one_head(): weights = jax.nn.softmax(scores, axis=-1).astype(jnp.bfloat16)]
  transfers between devices with their start and end apart: 5 -> 0, of which waited for: 5 -> 0; matrix products, arithmetic and copies ran while one was open for 28% -> 0% of each run, Pallas kernels for 0% -> 0%
where the time goes in v1:
time: 128 us; the launch traced here: 127 us
  Pallas kernels  120 us (94%)
  local copies, waits for them, and re-layouts  7.44 us (6%)
    pallas_call x1, Pallas kernels, on_device(): pl.pallas_call(kernel, out_shape=jax.ShapeDtypeStruct((ROWS, FEATS), BF16...  120 us
    unnamed x3, local copies, waits for them, and re-layouts  4.82 us

profile of v1, /device:TPU:2, one launch (start us, length us, event | category | flops | bytes accessed | tf_op | source)
XLA Modules:
  0.0 127.2 jit_solution(17987591395178090297)
XLA Ops:
  0.0 1.3 %reshape.28.gain_ref = bf16[4,1,1024]{2,1,0:T(2,128)(2,1)} reshape(bf16[4096]{0:T(1024)(128)(2,1)} %param.10) | data formatting | bytes 16384 | tf_op jit(solution)/shard_map/reshape | solution.py:623
  1.3 1.3 %reshape.29.router_ref = bf16[4,1,1024]{2,1,0:T(2,128)(2,1)} reshape(bf16[4096]{0:T(1024)(128)(2,1)} %param.11) | data formatting | bytes 16384 | tf_op jit(solution)/shard_map/reshape | solution.py:624
  2.6 1.4 %copy.12.blk_ref = s32[32,2]{1,0:T(8,128)} copy(s32[32,2]{0,1:T(2,128)} %param.17) | data formatting | bytes 512 | tf_op args[8]
  4.0 1.6 %copy.15.wo_ref = bf16[512,64]{1,0:T(8,128)(2,1)} copy(bf16[512,64]{0,1:T(8,128)(2,1)} %param.15) | data formatting | bytes 131072 | tf_op args[6]
  5.6 119.7 %depth_layer.1 = bf16[256,1024]{1,0:T(8,128)(2,1)} custom-call(s32[32]{0:T(128)} %seg_ref.1, s32[32,2]{1,0:T(8,128)} %copy.12.blk_ref, bf16[4,1,1024]{2,1,0:T(2,128)(2,1)} %reshape.28.gain_ref, bf16[4,1,1024]{2,1,0:T(2,128)(2,1)} %reshape.29.router_ref, bf16[16,128,1024]{2,1,0:T(8,128)(2,1)} %bitcast.5, bf16[4,1024,512]{2,1,0:T(8,128)(2,1)} %bitcast.6, ...), custom_call_target="tpu_custom_call" | custom-call | tf_op jit(solution)/shard_map/depth_layer/pallas_call | solution.py:578
  125.3 1.9 %copy.17 = bf16[2,128,1024]{2,1,0:T(8,128)(2,1)} copy(bf16[2,128,1024]{2,1,0:T(8,128)(2,1)} %bitcast.7) | data formatting | bytes 1048576

commit v2 on v1

--- a/solution.py
+++ b/solution.py
@@ -19,12 +19,12 @@
 QROWS = LOCAL_HEADS * BLK
 FEATS = 1024
 SEGS = 32
-KEY_SEGS = 4
-LOG2E = 1.4426950408889634
-Q_SCALE = LOG2E / (128.0**0.5)
+ACC = HD + 8
+KEY_SEGS = 8
+Q_SCALE = 1.0 / (128.0**0.5)
 MASKED = -1e30
 
-Y_FIRST = 96
+Y_FIRST = 64
 PY, PZ, RZ, RY, SIB, COPIES = 0, 4, 12, 20, 44, 56
 
 
@@ -32,8 +32,8 @@
     return jnp.dot(a, b, preferred_element_type=F32)
 
 
-def dot_t(a, b):
-    return lax.dot_general(a, b, (((1,), (1,)), ((), ())), preferred_element_type=F32)
+def dot_t0(a, b):
+    return lax.dot_general(a, b, (((0,), (0,)), ((), ())), preferred_element_type=F32)
 
 
 class Place:
@@ -243,15 +243,18 @@
     wk,
     wv,
     wkv,
+    gain,
+    router,
     xg0,
     xg1,
-    normed,
+    normed0,
+    normed1,
     wsend,
     wrecv,
     wg,
     kv0,
     kv1,
-    qx,
+    qt,
     acc,
     top,
     gates,
@@ -272,13 +275,18 @@
 ):
     me = Place()
     x, y, z, c = me.x, me.y, me.z, me.c
-    xg, hg = (xg0, xg1), (hg0, hg1)
+    xg, hg, normed = (xg0, xg1), (hg0, hg1), (normed0, normed1)
     tok_copy = pltpu.make_async_copy(tok_ref, tok, local_sems.at[0])
     wk_copy = pltpu.make_async_copy(wk_hbm, wk, local_sems.at[1])
     wv_copy = pltpu.make_async_copy(wv_hbm, wv, local_sems.at[2])
     wq_copy = pltpu.make_async_copy(wq_hbm, wq, local_sems.at[3])
     for copy in (tok_copy, wk_copy, wv_copy, wq_copy):
         copy.start()
+
+    for small, wide in ((gain_ref, gain), (router_ref, router)):
+        values = small[...].astype(F32)
+        for t in range(NX):
+            wide[t] = jnp.concatenate([values[t * 8 + i : t * 8 + i + 1] for i in range(8)], axis=1)
 
     sib = me.at(c=1 - c)
     barrier = pltpu.get_barrier_semaphore()
@@ -305,7 +313,7 @@
     there = lax.broadcasted_iota(jnp.int32, (64, 128), 0)
     spread = jnp.where(here == there + 64 * c, 1.0, 0.0).astype(BF16)
     for h in range(2):
-        wsend[h] = dot(wo_ref[h * 256 : (h + 1) * 256, :], spread).astype(BF16)
+        wsend[h] = dot_t0(wo_ref[:, h * 256 : (h + 1) * 256], spread).astype(BF16)
 
     own = me.s
 
@@ -316,8 +324,8 @@
         return (
             rank + jnp.where(seg < own, 1, 0),
             jnp.where(same, 1, hit),
-            jnp.where(same, blk_ref[j, 0], first),
-            jnp.where(same, blk_ref[j, 1], second),
+            jnp.where(same, blk_ref[0, j], first),
+            jnp.where(same, blk_ref[1, j], second),
         )
 
     zero = jnp.int32(0)
@@ -339,6 +347,7 @@
     x0 = ring_x(me, xg0, xcp, 0)
     x1 = ring_x(me, xg1, xcp, 4)
     run(x0, 1)
+    run(x1, 1)
 
     def w_copy(h, slot, device):
         return pltpu.make_async_remote_copy(
@@ -379,8 +388,9 @@
     run(gw, 3)
 
     run(x0, 1)
+    run(gw, 2)
     run(x1, 1)
-    run(gw, 2)
+    run(gw, 1)
 
     feat = [(x + d) % NX for d in range(NX)]
 
@@ -391,137 +401,134 @@
         for d in range(NX):
             part = xg[s][d].astype(F32)
             squares += jnp.sum(part * part, axis=1, keepdims=True)
-            routed += jnp.sum(part * router_ref[feat[d]].astype(F32), axis=1, keepdims=True)
+            routed += jnp.sum(part * router[feat[d]], axis=1, keepdims=True)
         scale = lax.rsqrt(squares * (1.0 / (NX * FEATS)) + 1e-05)
         gates[rows] = jax.nn.sigmoid(routed)
         for d in range(NX):
-            normed[d] = (xg[s][d].astype(F32) * scale * gain_ref[feat[d]].astype(F32)).astype(BF16)
-
-    def through(weight):
-        total = dot(normed[0], weight[feat[0]])
+            normed[s][d] = (xg[s][d].astype(F32) * scale * gain[feat[d]]).astype(BF16)
+
+    def through(s, weight):
+        total = dot(normed[s][0], weight[feat[0]])
         for d in range(1, NX):
-            total += dot(normed[d], weight[feat[d]])
+            total += dot(normed[s][d], weight[feat[d]])
         return total.astype(BF16)
 
-    def keys(kv):
-        found = through(wkv)
+    def keys(s, kv):
+        found = through(s, wkv)
         kv[0, 0, 0] = jnp.concatenate([found[:, 0:HD], found[:, HD : 2 * HD]], axis=0)
 
     def queries(s):
-        found = through(wq).astype(F32) * Q_SCALE
-        high = found.astype(BF16)
-        low = (found - high.astype(F32)).astype(BF16)
+        found = through(s, wq).astype(F32) * Q_SCALE
         for h in range(LOCAL_HEADS):
-            rows = slice(s * QROWS + h * BLK, s * QROWS + (h + 1) * BLK)
-            qx[rows, 0:HD] = high[:, h * HD : (h + 1) * HD]
-            qx[rows, HD : 2 * HD] = low[:, h * HD : (h + 1) * HD]
+            columns = slice(s * QROWS + h * BLK, s * QROWS + (h + 1) * BLK)
+            turned = found[:, h * HD : (h + 1) * HD].T
+            high = turned.astype(BF16)
+            qt[0:HD, columns] = high
+            qt[HD : 2 * HD, columns] = (turned - high.astype(F32)).astype(BF16)
 
     ones = jnp.ones((BLK, HD), BF16)
 
     def twice(key):
         return jnp.concatenate([key, key], axis=1)
 
-    run(x0)
-    norm(0)
-    keys(kv0)
-    g0 = gather_yz(me, kv0, Copies(g0_ss, g0_rs))
-    run(g0, 1)
-    wq_copy.wait()
-    queries(0)
-    run(g0, 2)
-    run(gw, 2)
-    run(x1, 1)
-    run(g0, 1)
-    run(gw, 2)
-    run(g0, 1)
-    run(gw, 2)
-    run(g0, 1)
-    run(gw)
-    run(x1)
-    norm(1)
-    keys(kv1)
-    g1 = gather_yz(me, kv1, Copies(g1_ss, g1_rs))
-    run(g1, 1)
-    run(g0, 1)
-    queries(1)
-    run(g0, 1)
-    run(g1, 1)
+    def weigh(scores, most, value_t):
+        return dot(value_t, jnp.exp(scores - most).astype(BF16))
+
+    def with_sum(value, mark):
+        return jnp.concatenate([value.T, mark], axis=0)
 
     def own_blocks():
         own0, own1 = kv0[0, 0, 0], kv1[0, 0, 0]
-        key0, value0 = own0[0:BLK], own0[BLK : 2 * BLK]
-        key1, value1 = own1[0:BLK], own1[BLK : 2 * BLK]
-        row = lax.broadcasted_iota(jnp.int32, (QROWS, BLK), 0) % BLK
-        column = lax.broadcasted_iota(jnp.int32, (QROWS, BLK), 1)
-        seen = column <= row
-        q0, q1 = qx[0:QROWS], qx[QROWS : 2 * QROWS]
-        s00 = jnp.where(seen, dot_t(q0, twice(key0)), MASKED)
-        most = jnp.max(s00, axis=1, keepdims=True)
-        top[0:QROWS] = most
-        acc[0:QROWS] = dot(
-            jnp.exp2(s00 - most).astype(BF16), jnp.concatenate([value0, ones], axis=1)
-        )
-        s10 = dot_t(q1, twice(key0))
-        s11 = jnp.where(seen, dot_t(q1, twice(key1)), MASKED)
-        most = jnp.max(jnp.maximum(s10, s11), axis=1, keepdims=True)
-        top[QROWS : 2 * QROWS] = most
-        acc[QROWS : 2 * QROWS] = dot(
-            jnp.exp2(s10 - most).astype(BF16), jnp.concatenate([value0, ones], axis=1)
-        ) + dot(jnp.exp2(s11 - most).astype(BF16), jnp.concatenate([value1, ones], axis=1))
-
-    own_blocks()
-    run(g0, 1)
-    run(g1, 2)
-    run(g0, 1)
-    run(g1, 1)
-    run(g0, 1)
-    run(g1, 1)
-    run(g0)
-
-    stand_in = jnp.broadcast_to(kv0[0, 0, 0][0:1], (BLK, HD))
+        key0, value0 = own0[0:BLK], with_sum(own0[BLK : 2 * BLK], ones)
+        key1, value1 = own1[0:BLK], with_sum(own1[BLK : 2 * BLK], ones)
+        key = lax.broadcasted_iota(jnp.int32, (BLK, QROWS), 0)
+        query = lax.broadcasted_iota(jnp.int32, (BLK, QROWS), 1) % BLK
+        seen = key <= query
+        columns = slice(0, QROWS)
+        s00 = jnp.where(seen, dot(twice(key0), qt[:, columns]), MASKED)
+        most = jnp.max(s00, axis=0, keepdims=True)
+        top[:, columns] = most
+        acc[:, columns] = weigh(s00, most, value0)[0:ACC]
+        columns = slice(QROWS, 2 * QROWS)
+        s10 = dot(twice(key0), qt[:, columns])
+        s11 = jnp.where(seen, dot(twice(key1), qt[:, columns]), MASKED)
+        most = jnp.max(jnp.maximum(s10, s11), axis=0, keepdims=True)
+        top[:, columns] = most
+        acc[:, columns] = (weigh(s10, most, value0) + weigh(s11, most, value1))[0:ACC]
+
     nothing = jnp.zeros((BLK, HD), BF16)
 
-    def attend(kv, chunk):
-        key_parts, value_parts = [], []
+    def attend(kv, chunk, stand_in):
+        key_parts, value_parts, marks = [], [], []
         for i in range(KEY_SEGS):
             j = chunk * KEY_SEGS + i
             home = seg_ref[j]
             block = kv[(home + c) & 1, ((home >> 4) + NY - y) & 3, ((home >> 1) + NZ - z) & 7]
             seen = j < rank
-            key_parts.append(twice(jnp.where(seen, block[0:BLK], stand_in)))
-            value_parts.append(
-                jnp.concatenate(
-                    [
-                        jnp.where(seen, block[BLK : 2 * BLK], nothing),
-                        jnp.where(seen, ones, nothing),
-                    ],
-                    axis=1,
-                )
-            )
-        key_chunk = jnp.concatenate(key_parts, axis=0)
-        value_chunk = jnp.concatenate(value_parts, axis=0)
+            key_parts.append(jnp.where(seen, block[0:BLK], stand_in))
+            value_parts.append(jnp.where(seen, block[BLK : 2 * BLK], nothing))
+            marks.append(jnp.where(seen, ones, nothing))
+        key_chunk = twice(jnp.concatenate(key_parts, axis=0))
+        value_t = with_sum(
+            jnp.concatenate(value_parts, axis=0), jnp.concatenate(marks, axis=1)
+        )
         tile = 256
         for t in range(2 * QROWS // tile):
-            rows = slice(t * tile, (t + 1) * tile)
-            scores = dot_t(qx[rows], key_chunk)
-            old = top[rows]
-            new = jnp.maximum(old, jnp.max(scores, axis=1, keepdims=True))
-            top[rows] = new
-            weights = jnp.exp2(scores - new).astype(BF16)
-            acc[rows] = acc[rows] * jnp.exp2(old - new) + dot(weights, value_chunk)
+            columns = slice(t * tile, (t + 1) * tile)
+            scores = dot(key_chunk, qt[:, columns])
+            old = top[:, columns]
+            new = jnp.maximum(old, jnp.max(scores, axis=0, keepdims=True))
+            top[:, columns] = new
+            acc[:, columns] = (
+                acc[:, columns] * jnp.exp(old - new) + weigh(scores, new, value_t)[0:ACC]
+            )
 
     def attend_some(kv, low, high):
+        stand_in = jnp.broadcast_to(kv0[0, 0, 0][0:1], (BLK, HD))
+
         def step(chunk, carry):
-            attend(kv, chunk)
+            attend(kv, chunk, stand_in)
             return carry
 
         lax.fori_loop(low, high, step, 0)
 
     chunks = SEGS // KEY_SEGS
-    for low in range(0, chunks, 2):
-        attend_some(kv0, low, low + 2)
+
+    run(x0)
+    norm(0)
+    keys(0, kv0)
+    g0 = gather_yz(me, kv0, Copies(g0_ss, g0_rs))
+    run(g0, 1)
+    run(gw, 2)
+    run(x1)
+    norm(1)
+    keys(1, kv1)
+    g1 = gather_yz(me, kv1, Copies(g1_ss, g1_rs))
+    run(g1, 1)
+    run(g0, 2)
+    run(gw, 1)
+    wq_copy.wait()
+    queries(0)
+    run(g1, 2)
+    run(g0, 1)
+    run(gw, 1)
+    queries(1)
+    run(g0, 1)
+    run(g1, 1)
+    run(gw, 1)
+    own_blocks()
+    run(g0, 1)
+    run(gw, 1)
+    for _ in range(4):
+        run(g0, 1)
+        run(g1, 1)
+        run(gw, 1)
+    run(g0)
+    for low in range(chunks):
+        attend_some(kv0, low, low + 1)
         run(g1, 2)
     run(g1)
+    run(gw)
     attend_some(kv1, 0, chunks)
 
     h0 = ring_x(me, hg0, xcp, 8)
@@ -530,8 +537,8 @@
     def finish(s):
         parts = []
         for h in range(LOCAL_HEADS):
-            rows = slice(s * QROWS + h * BLK, s * QROWS + (h + 1) * BLK)
-            parts.append((acc[rows, 0:HD] / acc[rows, HD : 2 * HD]).astype(BF16))
+            columns = slice(s * QROWS + h * BLK, s * QROWS + (h + 1) * BLK)
+            parts.append((acc[0:HD, columns] / acc[HD : HD + 1, columns]).T.astype(BF16))
         hg[s][0] = jnp.concatenate(parts, axis=1)
 
     finish(0)
@@ -586,6 +593,9 @@
             pltpu.VMEM((NX, FEATS, HD), BF16),
             pltpu.VMEM((NX, FEATS, HD), BF16),
             pltpu.VMEM((NX, FEATS, 2 * HD), BF16),
+            pltpu.VMEM((NX, 1, FEATS), F32),
+            pltpu.VMEM((NX, 1, FEATS), F32),
+            pltpu.VMEM((NX, BLK, FEATS), BF16),
             pltpu.VMEM((NX, BLK, FEATS), BF16),
             pltpu.VMEM((NX, BLK, FEATS), BF16),
             pltpu.VMEM((NX, BLK, FEATS), BF16),
@@ -594,9 +604,9 @@
             pltpu.VMEM((2, NY, NZ, 256, 128), BF16),
             pltpu.VMEM((2, NY, NZ, 256, 128), BF16),
             pltpu.VMEM((2, NY, NZ, 256, 128), BF16),
-            pltpu.VMEM((2 * QROWS, 2 * HD), BF16),
-            pltpu.VMEM((2 * QROWS, 2 * HD), F32),
-            pltpu.VMEM((2 * QROWS, 1), F32),
+            pltpu.VMEM((2 * HD, 2 * QROWS), BF16),
+            pltpu.VMEM((ACC, 2 * QROWS), F32),
+            pltpu.VMEM((1, 2 * QROWS), F32),
             pltpu.VMEM((ROWS, 1), F32),
             pltpu.VMEM((NX, BLK, 512), BF16),
             pltpu.VMEM((NX, BLK, 512), BF16),
@@ -619,14 +629,14 @@
         name="depth_layer",
     )(
         seg_ids,
-        blk_ids,
-        norm_gain.reshape(NX, 1, FEATS),
-        router_weight.reshape(NX, 1, FEATS),
+        blk_ids.T,
+        norm_gain.reshape(NX * 8, HD),
+        router_weight.reshape(NX * 8, HD),
         tokens.reshape(16, BLK, FEATS),
         w_query.reshape(NX, FEATS, 512),
         w_key.reshape(NX, FEATS, HD),
         w_value.reshape(NX, FEATS, HD),
-        w_out,
+        w_out.T,
     )
     return new_rows.reshape(2, BLK, FEATS)
 

time: 128 us -> 117 us (0.914)
  local copies, waits for them, and re-layouts: 7.44 us -> 1.87 us
  Pallas kernels: 120 us -> 115 us
    pallas_call x1, Pallas kernels: 120 us -> 115 us  [on_device(): pl.pallas_call(kernel, out_shape=jax.ShapeDtypeStruct((ROWS, FEATS), BF16...]
    unnamed x3 -> x1, local copies, waits for them, and re-layouts: 4.82 us -> 1.87 us
    reshape x2 -> x0, local copies, waits for them, and re-layouts: 2.62 us -> none  [the longest x1 1.31 us: on_device(): router_weight.reshape(NX, 1, FEATS)]
where the time goes in v2:
time: 117 us; the launch traced here: 116 us
  Pallas kernels  115 us (98%)
  local copies, waits for them, and re-layouts  1.87 us (2%)
    pallas_call x1, Pallas kernels, on_device(): pl.pallas_call(kernel, out_shape=jax.ShapeDtypeStruct((ROWS, FEATS), BF16...  115 us

profile of v2, /device:TPU:2, one launch (start us, length us, event | category | flops | bytes accessed | tf_op | source)
XLA Modules:
  0.0 116.5 jit_solution(8466237728357540776)
XLA Ops:
  0.0 114.6 %depth_layer.1 = bf16[256,1024]{1,0:T(8,128)(2,1)} custom-call(s32[32]{0:T(128)} %seg_ref.1, s32[2,32]{1,0:T(2,128)} %bitcast.17, bf16[32,128]{1,0:T(8,128)(2,1)} %bitcast.15, bf16[32,128]{1,0:T(8,128)(2,1)} %bitcast.16, bf16[16,128,1024]{2,1,0:T(8,128)(2,1)} %bitcast.9, bf16[4,1024,512]{2,1,0:T(8,128)(2,1)} %bitcast.10, bf16[4,1024,128]{2,1,0:T(8,128)(2,1)} %bitcast.12, ...), custom_call_target="tpu_custom_call" | custom-call | tf_op jit(solution)/shard_map/depth_layer/pallas_call | solution.py:585
  114.6 1.9 %copy.11 = bf16[2,128,1024]{2,1,0:T(8,128)(2,1)} copy(bf16[2,128,1024]{2,1,0:T(8,128)(2,1)} %bitcast.11) | data formatting | bytes 1048576

commit v3 on v2

--- a/solution.py
+++ b/solution.py
@@ -415,7 +415,9 @@
 
     def keys(s, kv):
         found = through(s, wkv)
-        kv[0, 0, 0] = jnp.concatenate([found[:, 0:HD], found[:, HD : 2 * HD]], axis=0)
+        kv[0, 0, 0] = jnp.concatenate(
+            [found[:, 0:HD], found[:, HD : 2 * HD].astype(F32).T.astype(BF16)], axis=0
+        )
 
     def queries(s):
         found = through(s, wq).astype(F32) * Q_SCALE
@@ -435,7 +437,7 @@
         return dot(value_t, jnp.exp(scores - most).astype(BF16))
 
     def with_sum(value, mark):
-        return jnp.concatenate([value.T, mark], axis=0)
+        return jnp.concatenate([value, mark], axis=0)
 
     def own_blocks():
         own0, own1 = kv0[0, 0, 0], kv1[0, 0, 0]
@@ -470,7 +472,7 @@
             marks.append(jnp.where(seen, ones, nothing))
         key_chunk = twice(jnp.concatenate(key_parts, axis=0))
         value_t = with_sum(
-            jnp.concatenate(value_parts, axis=0), jnp.concatenate(marks, axis=1)
+            jnp.concatenate(value_parts, axis=1), jnp.concatenate(marks, axis=1)
         )
         tile = 256
         for t in range(2 * QROWS // tile):
@@ -499,6 +501,8 @@
     keys(0, kv0)
     g0 = gather_yz(me, kv0, Copies(g0_ss, g0_rs))
     run(g0, 1)
+    wq_copy.wait()
+    queries(0)
     run(gw, 2)
     run(x1)
     norm(1)
@@ -507,8 +511,6 @@
     run(g1, 1)
     run(g0, 2)
     run(gw, 1)
-    wq_copy.wait()
-    queries(0)
     run(g1, 2)
     run(g0, 1)
     run(gw, 1)
@@ -516,13 +518,13 @@
     run(g0, 1)
     run(g1, 1)
     run(gw, 1)
-    own_blocks()
     run(g0, 1)
     run(gw, 1)
     for _ in range(4):
         run(g0, 1)
         run(g1, 1)
         run(gw, 1)
+    own_blocks()
     run(g0)
     for low in range(chunks):
         attend_some(kv0, low, low + 1)

time: 117 us -> 117 us (level)
  no operation moved by 1% of the time
where the time goes in v3:
time: 117 us; the launch traced here: 116 us
  Pallas kernels  114 us (97%)
  local copies, waits for them, and re-layouts  1.87 us (2%)
    pallas_call x1, Pallas kernels, on_device(): pl.pallas_call(kernel, out_shape=jax.ShapeDtypeStruct((ROWS, FEATS), BF16...  114 us

profile of v3, /device:TPU:2, one launch (start us, length us, event | category | flops | bytes accessed | tf_op | source)
XLA Modules:
  0.0 116.2 jit_solution(7164847105291315841)
XLA Ops:
  0.0 114.4 %depth_layer.1 = bf16[256,1024]{1,0:T(8,128)(2,1)} custom-call(s32[32]{0:T(128)} %seg_ref.1, s32[2,32]{1,0:T(2,128)} %bitcast.17, bf16[32,128]{1,0:T(8,128)(2,1)} %bitcast.15, bf16[32,128]{1,0:T(8,128)(2,1)} %bitcast.16, bf16[16,128,1024]{2,1,0:T(8,128)(2,1)} %bitcast.9, bf16[4,1024,512]{2,1,0:T(8,128)(2,1)} %bitcast.10, bf16[4,1024,128]{2,1,0:T(8,128)(2,1)} %bitcast.12, ...), custom_call_target="tpu_custom_call" | custom-call | tf_op jit(solution)/shard_map/depth_layer/pallas_call | solution.py:587
  114.4 1.9 %copy.11 = bf16[2,128,1024]{2,1,0:T(8,128)(2,1)} copy(bf16[2,128,1024]{2,1,0:T(8,128)(2,1)} %bitcast.11) | data formatting | bytes 1048576

commit v4 on v3

--- a/solution.py
+++ b/solution.py
@@ -25,7 +25,7 @@
 MASKED = -1e30
 
 Y_FIRST = 64
-PY, PZ, RZ, RY, SIB, COPIES = 0, 4, 12, 20, 44, 56
+PY, PZ, RZ, RY, SIB, COPIES = 0, 4, 12, 20, 44, 63
 
 
 def dot(a, b):
@@ -196,9 +196,10 @@
     sib_col(7, 4)
     for j in range(8):
         cp.recv(RY + 16 + j)
-    sib_row(3, 2)
-    yield
-    for j in range(12):
+        far = r(order[j], 2)
+        cp.send(far, other.at[2, order[j], Y_FIRST:256], SIB + 11 + j, sib)
+    yield
+    for j in range(19):
         cp.recv(SIB + j)
     cp.drain()
 
@@ -388,7 +389,6 @@
     run(gw, 3)
 
     run(x0, 1)
-    run(gw, 2)
     run(x1, 1)
     run(gw, 1)
 
@@ -503,14 +503,13 @@
     run(g0, 1)
     wq_copy.wait()
     queries(0)
-    run(gw, 2)
     run(x1)
     norm(1)
     keys(1, kv1)
     g1 = gather_yz(me, kv1, Copies(g1_ss, g1_rs))
     run(g1, 1)
     run(g0, 2)
-    run(gw, 1)
+    run(gw, 3)
     run(g1, 2)
     run(g0, 1)
     run(gw, 1)

time: 117 us -> 121 us (1.034)
  Pallas kernels: 114 us -> 119 us
    pallas_call x1, Pallas kernels: 114 us -> 119 us  [on_device(): pl.pallas_call(kernel, out_shape=jax.ShapeDtypeStruct((ROWS, FEATS), BF16...]
where the time goes in v4:
time: 121 us
  Pallas kernels  119 us (98%)
  local copies, waits for them, and re-layouts  1.87 us (2%)
    pallas_call x1, Pallas kernels, on_device(): pl.pallas_call(kernel, out_shape=jax.ShapeDtypeStruct((ROWS, FEATS), BF16...  119 us

profile of v4, /device:TPU:2, one launch (start us, length us, event | category | flops | bytes accessed | tf_op | source)
XLA Modules:
  0.0 121.1 jit_solution(17007721714803103092)
XLA Ops:
  0.0 119.3 %depth_layer.1 = bf16[256,1024]{1,0:T(8,128)(2,1)} custom-call(s32[32]{0:T(128)} %seg_ref.1, s32[2,32]{1,0:T(2,128)} %bitcast.17, bf16[32,128]{1,0:T(8,128)(2,1)} %bitcast.15, bf16[32,128]{1,0:T(8,128)(2,1)} %bitcast.16, bf16[16,128,1024]{2,1,0:T(8,128)(2,1)} %bitcast.9, bf16[4,1024,512]{2,1,0:T(8,128)(2,1)} %bitcast.10, bf16[4,1024,128]{2,1,0:T(8,128)(2,1)} %bitcast.12, ...), custom_call_target="tpu_custom_call" | custom-call | tf_op jit(solution)/shard_map/depth_layer/pallas_call | solution.py:586
  119.3 1.9 %copy.11 = bf16[2,128,1024]{2,1,0:T(8,128)(2,1)} copy(bf16[2,128,1024]{2,1,0:T(8,128)(2,1)} %bitcast.11) | data formatting | bytes 1048576
